TPU v7x, 32 devices: a whole 2x2x4 slice. The times are simulated.
32 devices in a mesh: groups: 2 (over y), dp: 4 (over z), tensor: 4 (over x, core).
Axes of the slice: x: 2, y: 2, z: 4, core: 2. Of those that a mesh axis runs over, the one named last changes fastest.
Arguments:
- hidden_in: bfloat16 [4096, 8192], P(('groups', 'dp'), 'tensor'), parts along dimension 0, may hold values from -6 to 6
- norm_gain: float32 [8192], replicated, may hold values from 0.25 to 1.75
- w_query: bfloat16 [8192, 4096], P(None, 'tensor')
- w_keyval: bfloat16 [8192, 1024], P('tensor')
- w_out: bfloat16 [4096, 8192], P('tensor'), may hold values from -0.125 to 0.125
- hyp_ids: int32 [4096], P(('groups', 'dp')), parts along dimension 0, may hold values from -1 to 20, as said below
Outputs:
- mixed: bfloat16 [4096, 8192], P(('groups', 'dp'), 'tensor'), parts along dimension 0
There are 2 independent parts, one for each index of `groups`. A program takes and returns all parts, laid end to end along the dimension named above; an argument that names none is the same for every part. Nothing has to cross between parts.
Inputs may be any that keep to these rules, and one draw needn't show every extreme that they name: `hyp_ids`: within each block of 512 rows of one dp index the numbers start at 0 and rise by one at each new hypothesis; padding rows (-1) only end a block; some block has no padding and holds 21 hypotheses.
All inputs are finite; a program needn't handle non-finite values.
Results may differ from a plain program's by a relative error of at most 0.0055.
Values may be sent and summed in bfloat16 or wider, within the bound.
A program may use at most 128 MiB of HBM per device.

v0:
```python
import jax
import jax.numpy as jnp
from jax import lax
from jax.sharding import PartitionSpec as P

D = 8192
HEADS = 32
KVH = 4
HD = 128


def positions(ids):
    rows = ids.shape[0]
    row = jnp.arange(rows, dtype=jnp.int32)
    prev = jnp.concatenate([jnp.full((1,), -2, jnp.int32), ids[:-1]])
    start = jnp.where(ids != prev, row, jnp.zeros_like(row))
    start = lax.cummax(start, axis=0)
    return (row - start).astype(jnp.float32)


def rotate(heads, pos):
    half = heads.shape[-1] // 2
    freq = 500000.0 ** (-jnp.arange(half, dtype=jnp.float32) * 2.0 / heads.shape[-1])
    angle = pos[:, None] * freq[None, :]
    cosine = jnp.cos(angle)[:, None, :]
    sine = jnp.sin(angle)[:, None, :]
    first = heads[..., :half]
    second = heads[..., half:]
    return jnp.concatenate(
        [first * cosine - second * sine, second * cosine + first * sine], axis=-1
    )


def shards(hidden_in, norm_gain, w_query, w_keyval, w_out, hyp_ids):
    rows = hidden_in.shape[0]
    local_width = hidden_in.shape[1]
    shard = lax.axis_index("tensor")
    local_gain = lax.dynamic_slice_in_dim(norm_gain, shard * local_width, local_width)
    local_normed = (hidden_in.astype(jnp.float32) * local_gain[None, :]).astype(jnp.bfloat16)
    kv_term = jnp.dot(local_normed, w_keyval, preferred_element_type=jnp.float32)
    keyval = lax.psum(kv_term, "tensor")
    whole = lax.all_gather(hidden_in, "tensor", axis=1, tiled=True)
    wide = whole.astype(jnp.float32)
    squares = jnp.sum(wide * wide, axis=-1)
    normed = (wide * norm_gain[None, :]).astype(jnp.bfloat16)
    query_raw = jnp.dot(normed, w_query, preferred_element_type=jnp.float32)
    scale = lax.rsqrt(squares / D + 1e-05)
    pos = positions(hyp_ids)
    local_heads = w_query.shape[1] // HD
    query = rotate((query_raw * scale[:, None]).reshape(rows, local_heads, HD), pos).astype(
        jnp.bfloat16
    )
    keyval = keyval * scale[:, None]
    keys = rotate(keyval[:, : KVH * HD].reshape(rows, KVH, HD), pos)
    values = keyval[:, KVH * HD :].reshape(rows, KVH, HD)
    group = HEADS // KVH
    head_index = shard * local_heads + jnp.arange(local_heads, dtype=jnp.int32)
    select = (head_index[:, None] // group == jnp.arange(KVH, dtype=jnp.int32)[None, :]).astype(
        jnp.float32
    )
    keys = jnp.einsum("tgd,hg->thd", keys.astype(jnp.bfloat16).astype(jnp.float32), select).astype(
        jnp.bfloat16
    )
    values = jnp.einsum(
        "tgd,hg->thd", values.astype(jnp.bfloat16).astype(jnp.float32), select
    ).astype(jnp.bfloat16)
    row = jnp.arange(rows, dtype=jnp.int32)
    allowed = (
        (hyp_ids[:, None] == hyp_ids[None, :])
        & (hyp_ids[:, None] >= 0)
        & (row[None, :] <= row[:, None])
    )
    scores = jnp.einsum("qhd,khd->hqk", query, keys, preferred_element_type=jnp.float32) / jnp.sqrt(
        jnp.float32(HD)
    )
    scores = jnp.where(allowed[None], scores, jnp.float32(-1e30))
    peak = jnp.max(scores, axis=-1, keepdims=True)
    expo = jnp.where(allowed[None], jnp.exp(scores - peak), jnp.float32(0.0))
    total = jnp.maximum(jnp.sum(expo, axis=-1, keepdims=True), 1.0)
    probs = (expo / total).astype(jnp.bfloat16)
    context = jnp.einsum("hqk,khd->qhd", probs, values, preferred_element_type=jnp.float32)
    context = context.astype(jnp.bfloat16).reshape(rows, local_heads * HD)
    out_term = jnp.dot(context, w_out, preferred_element_type=jnp.float32)
    summed = lax.psum_scatter(out_term, "tensor", scatter_dimension=1, tiled=True)
    return (hidden_in.astype(jnp.float32) + summed).astype(jnp.bfloat16)


def solution(mesh):
    return jax.shard_map(
        shards,
        mesh=mesh,
        in_specs=(
            P(("groups", "dp"), "tensor"),
            P(),
            P(None, "tensor"),
            P("tensor", None),
            P("tensor", None),
            P(("groups", "dp")),
        ),
        out_specs=P(("groups", "dp"), "tensor"),
        check_vma=False,
    )
```

profile of v0, /device:TPU:0, one launch (start us, length us, event | category | flops | bytes accessed | tf_op | source)
XLA Modules:
  0.0 316.9 jit_solution(12183220346616102736)
XLA Ops:
  6.5 0.0 all-gather.2.cloned.1.call-start
  6.5 0.7 all-gather.2.cloned.1.call-update
  7.3 0.0 all-reduce.2.cloned.1.call-start
  7.3 0.7 dynamic_slice.3
  8.0 6.5 %fusion.13 = f32[512,1024]{1,0:T(8,128)} fusion(bf16[2048,1024]{1,0:T(8,128)(2,1)} %param.9, bf16[512,2048]{1,0:T(8,128)(2,1)} %param.6, f32[2048]{0:T(1024)S(1)} %dynamic_slice.3), kind=kOutput, calls=%fused_computation.19 | convolution fusion | flops 2150629376 | bytes 8396800 | tf_op jit(solution)/shard_map/dot_general | solution.py:40
  14.5 0.0 all-reduce.2.cloned.1.call-update
  14.5 0.0 reduce-scatter.2.cloned.1.call-start
  14.6 0.0 copy-done.4
  14.6 0.1 select_bitcast_fusion
  14.7 0.3 reduce-window.9
  15.0 0.1 slice.32
  15.1 0.1 slice_reduce_fusion
  15.2 0.1 fusion.36
  15.3 1.7 multiply_cosine_fusion
  17.1 0.9 fusion.27
  18.0 52.0 %all-gather.2.cloned.1.call-done = bf16[512,8192]{1,0:T(8,128)(2,1)} async-done(((bf16[512,2048]{1,0:T(8,128)(2,1)}), bf16[512,8192]{1,0:T(8,128)(2,1)}) %all-gather.2.cloned.1.call-update) | async-done | bytes 8388624 | tf_op jit(solution)/shard_map/all_gather | solution.py:42
  69.9 5.1 %fusion.1 = f32[512]{0:T(512)S(1)} fusion(bf16[512,8192]{1,0:T(8,128)(2,1)} %all-gather.2.cloned.1.call-done), kind=kLoop, calls=%fused_computation.3 | loop fusion | flops 12582400 | bytes 8390656 | tf_op jit(solution)/shard_map/reduce_sum | solution.py:44
  75.1 48.6 %all-reduce.2.cloned.1.call-done = f32[512,1024]{1,0:T(8,128)} async-done(((f32[512,1024]{1,0:T(8,128)}), f32[512,1024]{1,0:T(8,128)}) %all-reduce.2.cloned.1.call-update) | async-done | bytes 2097168 | tf_op jit(solution)/shard_map/psum | solution.py:41
  123.7 1.8 broadcast_multiply_fusion
  125.5 0.9 slice.50
  126.4 1.1 slice.41
  127.5 0.0 copy-done.5
  127.5 14.6 %multiply_bitcast_fusion = f32[64,8,8,128]{3,1,2,0:T(8,128)S(1)} fusion(bf16[8192,1024]{1,0:T(8,128)(2,1)} %param.8, bf16[512,8192]{1,0:T(8,128)(2,1)} %all-gather.2.cloned.1.call-done, f32[8192]{0:T(1024)S(1)} %copy-done.5, f32[512]{0:T(512)S(1)} %add_rsqrt_fusion), kind=kOutput, calls=%fused_computation.23 | convolution fusion | flops 8603041792 | bytes 27297792 | tf_op jit(solution)/shard_map/dot_general | solution.py:46
  142.1 0.5 copy.18
  142.5 1.6 reshape.197
  144.1 2.0 convert_element_type.56
  146.1 2.5 fusion.34
  148.6 2.4 copy.13
  151.0 0.7 fusion.43
  151.7 0.3 copy-done.1
  152.0 0.8 subtract_convert_fusion.1
  152.8 0.8 fusion.28
  153.6 0.8 subtract_convert_fusion
  154.4 0.0 copy-start.3
  154.4 1.3 fusion.20
  155.7 0.0 copy-done.3
  155.8 0.0 slice-start
  155.8 0.0 slice-start.1
  155.8 6.5 %fusion.44 = (f32[8,512]{1,0:T(8,128)S(1)}, f32[8,512,512]{1,2,0:T(8,128)}) fusion(f32[8,512,512]{1,2,0:T(8,128)S(1)} %fusion.20, pred[512,512]{0,1:T(8,128)(4,1)S(1)} %copy-done.3), kind=kOutput, calls=%fused_computation.68 | output fusion | flops 14680575 | bytes 17055744 | tf_op jit(solution)/shard_map/sub | solution.py:78
  162.3 0.0 copy-done.2
  162.3 0.0 slice-start.3
  162.3 4.3 %fusion.18 = bf16[8,128,512]{2,1,0:T(8,128)(2,1)S(1)} fusion(f32[8,512,512]{1,2,0:T(8,128)} %get-tuple-element.14, f32[8,512]{1,0:T(8,128)S(1)} %broadcast_maximum_fusion, bf16[8,512,128]{1,2,0:T(8,128)(2,1)S(1)} %copy-done.2), kind=kOutput, calls=%fused_computation.25 | convolution fusion | flops 541589504 | bytes 10502144 | tf_op jit(solution)/shard_map/hqk,khd->qhd/dot_general | solution.py:81
  166.6 0.3 slice-done.2
  166.8 1.3 slice-done.3
  168.1 11.7 %fusion.45 = f32[512,8192]{1,0:T(8,128)} fusion(bf16[512,1024]{0,1:T(8,128)(2,1)S(1)} %bitcast.31, bf16[1024,8192]{1,0:T(8,128)(2,1)S(1)} %bitcast.30), kind=kOutput, calls=%fused_computation.69 | convolution fusion | flops 8589934592 | bytes 34603008 | tf_op jit(solution)/shard_map/dot_general | solution.py:83
  179.9 0.0 reduce-scatter.2.cloned.1.call-update
  179.9 126.3 %reduce-scatter.2.cloned.1.call-done = f32[512,2048]{1,0:T(8,128)} async-done(((f32[512,8192]{1,0:T(8,128)}), f32[512,2048]{1,0:T(8,128)}) %reduce-scatter.2.cloned.1.call-update) | async-done | bytes 4194320 | tf_op jit(solution)/shard_map/reduce_scatter | solution.py:84
  306.2 4.2 %fusion.8 = bf16[512,2048]{1,0:T(8,128)(2,1)} fusion(f32[512,2048]{1,0:T(8,128)} %reduce-scatter.2.cloned.1.call-done, bf16[512,2048]{1,0:T(8,128)(2,1)S(1)} %copy-done), kind=kLoop, calls=%fused_computation.14 | loop fusion | flops 3145728 | bytes 8388608 | tf_op jit(solution)/shard_map/convert_element_type | solution.py:85
  (16 shorter events, 0.1 us)
Async XLA Ops:
  6.5 63.4 %all-gather.2.cloned.1.call-start = ((), (), s32[]{:S(2)}) async-start(), calls=%async_computation.2 | async-start | bytes 10485760 | tf_op jit(solution)/shard_map/all_gather | solution.py:42
  7.3 116.5 %all-reduce.2.cloned.1.call-start = ((), (), s32[]{:S(2)}) async-start(), calls=%async_computation.1 | async-start | bytes 4194304 | tf_op jit(solution)/shard_map/psum | solution.py:41
  8.0 6.6 %copy-start.4 = (s32[512]{0:T(512)S(1)}, s32[512]{0:T(512)}, u32[]{:S(2)}) copy-start(s32[512]{0:T(512)} %param.11) | copy-start | bytes 6148
  14.5 291.7 %reduce-scatter.2.cloned.1.call-start = ((), (), s32[]{:S(2)}) async-start(), calls=%async_computation.3 | async-start | bytes 20971520 | tf_op jit(solution)/shard_map/reduce_scatter | solution.py:84
  75.1 52.5 %copy-start.5 = (f32[8192]{0:T(1024)S(1)}, f32[8192]{0:T(1024)}, u32[]{:S(2)}) copy-start(f32[8192]{0:T(1024)} %param.7) | copy-start | bytes 98308
  151.0 0.9 copy-start.1
  154.4 1.4 copy-start.3
  155.7 6.5 %copy-start.2 = (bf16[8,512,128]{1,2,0:T(8,128)(2,1)S(1)}, bf16[8,512,128]{1,2,0:T(8,128)(2,1)}, u32[]{:S(2)}) copy-start(bf16[8,512,128]{1,2,0:T(8,128)(2,1)} %copy.13) | copy-start | bytes 3145732
  155.8 10.8 %slice-start = ((s8[16777216]{0:T(1024)(128)(4,1)}), s8[4194304]{0:T(1024)(128)(4,1)S(1)}, s32[]{:S(2)}) async-start(s8[16777216]{0:T(1024)(128)(4,1)} %bitcast.29), calls=%async_computation.4 | async-start | bytes 8388608
  155.8 10.8 %slice-start.1 = ((s8[16777216]{0:T(1024)(128)(4,1)}), s8[4194304]{0:T(1024)(128)(4,1)S(1)}, s32[]{:S(2)}) async-start(s8[16777216]{0:T(1024)(128)(4,1)} %bitcast.29), calls=%async_computation.5 | async-start | bytes 8388608
  162.3 4.6 %slice-start.2 = ((s8[16777216]{0:T(1024)(128)(4,1)}), s8[4194304]{0:T(1024)(128)(4,1)S(1)}, s32[]{:S(2)}) async-start(s8[16777216]{0:T(1024)(128)(4,1)} %bitcast.29), calls=%async_computation.6 | async-start | bytes 8388608
  162.3 5.8 %slice-start.3 = ((s8[16777216]{0:T(1024)(128)(4,1)}), s8[4194304]{0:T(1024)(128)(4,1)S(1)}, s32[]{:S(2)}) async-start(s8[16777216]{0:T(1024)(128)(4,1)} %bitcast.29), calls=%async_computation.7 | async-start | bytes 8388608
  179.9 126.4 %copy-start = (bf16[512,2048]{1,0:T(8,128)(2,1)S(1)}, bf16[512,2048]{1,0:T(8,128)(2,1)}, u32[]{:S(2)}) copy-start(bf16[512,2048]{1,0:T(8,128)(2,1)} %param.6) | copy-start | bytes 6291460
Sparse Core Ops, SparseCore 0:
  8.9 60.9 all-gather.1
  72.3 51.3 all-reduce.1
  180.0 126.1 reduce-scatter.1
where the time goes:
time: 317 us
  waiting for transfers between devices  228 us (72%)
  matrix products  41.7 us (13%)
  other arithmetic  22.4 us (7%)
  between operations  13.3 us (4%)
  local copies, waits for them, and re-layouts  11.9 us (4%)
    reduce_scatter x1, waiting for transfers between devices, shards(): lax.psum_scatter(out_term, 'tensor', scatter_dimension=1, tiled=True)  126 us
    all_gather x1, waiting for transfers between devices, shards(): whole = lax.all_gather(hidden_in, 'tensor', axis=1, tiled=True)  52 us
    psum x1, waiting for transfers between devices, shards(): keyval = lax.psum(kv_term, 'tensor')  48.6 us
    dot_general x1, matrix products, shards(): query_raw = jnp.dot(normed, w_query, preferred_element_type=jnp.float32)  14.6 us
    dot_general x1, matrix products, shards(): out_term = jnp.dot(context, w_out, preferred_element_type=jnp.float32)  11.7 us
    sub x1, other arithmetic, shards(): expo = jnp.where(allowed[None], jnp.exp(scores - peak), jnp.float32(0.0))  6.48 us
    dot_general x1, matrix products, shards(): jnp.dot(local_normed, w_keyval, preferred_element_type=jnp.float32)  6.48 us
  transfers between devices with their start and end apart: 3, of which 3 were waited for; matrix products, arithmetic and copies ran while one was open for 5% of the time, Pallas kernels for 0%

commit v1 on v0

--- a/solution.py
+++ b/solution.py
@@ -1,12 +1,356 @@
+import functools
+
 import jax
 import jax.numpy as jnp
+import numpy as np
 from jax import lax
+from jax.experimental import pallas as pl
+from jax.experimental.pallas import tpu as pltpu
 from jax.sharding import PartitionSpec as P
 
 D = 8192
 HEADS = 32
 KVH = 4
 HD = 128
+CHUNKS = 4
+MESH = pl.DeviceIdType.MESH
+F32 = jnp.float32
+BF16 = jnp.bfloat16
+
+
+def turn(v, cosine, sine):
+    return v * cosine + pltpu.roll(v, HD // 2, 1) * sine
+
+
+def kernel(
+    hid, gain, freq, sign, ids, wq_h, wkv_h, wo_h, out,
+    g, wq, wo, nrm, kvp, kvr, kxs, kxr, kbuf, vbuf, qbuf, ctx,
+    a_out, b_out, x_out, a_in, b_in, x_in, acc,
+    agx_s, agc_s, fwd_s, g1_r, g2_r, g3_r, kv_s, kv_r,
+    a_s, b_s, x_s, a_r, b_r, x_r, l_hid, l_kv, l_wq, l_wo, l_out,
+):
+    rows, width = hid.shape
+    R = rows // CHUNKS
+    heads = wq_h.shape[1] // HD
+    half = wkv_h.shape[0] // 2
+    me = lax.axis_index("tensor")
+    chip, core = me // 2, me % 2
+    d1 = chip * 2 + (1 - core)
+    d2 = (1 - chip) * 2 + core
+    d3 = 3 - me
+    dev = (me, d1, d2, d3)
+
+    barrier = pltpu.get_barrier_semaphore()
+    for other in (d1, d2):
+        pl.semaphore_signal(barrier, inc=1, device_id={"tensor": other}, device_id_type=MESH)
+
+    own_copy = pltpu.make_async_copy(hid, g.at[0], l_hid.at[0])
+    own_copy.start()
+    kv_copies = []
+    for r in range(4):
+        for which in range(2):
+            for h in range(2):
+                col = pl.multiple_of(which * (KVH * HD) + dev[r] * HD, HD)
+                kv_copies.append(
+                    pltpu.make_async_copy(
+                        wkv_h.at[pl.ds(h * half, half), pl.ds(col, HD)],
+                        wo.at[0, :, pl.ds(h * 1024 + r * 256 + which * HD, HD)],
+                        l_kv.at[(r * 2 + which) * 2 + h],
+                    )
+                )
+    for copy in kv_copies:
+        copy.start()
+
+    pl.semaphore_wait(barrier, 2)
+
+    def rows_of(c):
+        return pl.ds(pl.multiple_of(c * R, R), R)
+
+    def remote(src, dst, send, recv, to):
+        return pltpu.make_async_remote_copy(
+            src_ref=src, dst_ref=dst, send_sem=send, recv_sem=recv,
+            device_id={"tensor": to}, device_id_type=MESH,
+        )
+
+    def gather_x(c):
+        return remote(hid.at[rows_of(c), :], g.at[2, rows_of(c), :], agx_s.at[c], g2_r.at[c], d2)
+
+    def gather_core(c):
+        return remote(hid.at[rows_of(c), :], g.at[1, rows_of(c), :], agc_s.at[c], g1_r.at[c], d1)
+
+    def forward(c):
+        return remote(
+            g.at[2, rows_of(c), :], g.at[3, rows_of(c), :], fwd_s.at[c], g3_r.at[c], d1
+        )
+
+    for c in range(2):
+        gather_x(c).start()
+        gather_core(c).start()
+
+    wq_copies = [
+        pltpu.make_async_copy(
+            wq_h.at[pl.ds(pl.multiple_of(dev[r] * width, width), width), :], wq.at[r], l_wq.at[r]
+        )
+        for r in range(4)
+    ]
+    wo_copies = [
+        pltpu.make_async_copy(
+            wo_h.at[:, pl.ds(pl.multiple_of(dev[r] * width, width), width)], wo.at[r], l_wo.at[r]
+        )
+        for r in range(4)
+    ]
+    for copy in wq_copies:
+        copy.start()
+    for r in (3, 1, 2):
+        wo_copies[r].start()
+
+    kbuf[...] = jnp.zeros_like(kbuf)
+    vbuf[...] = jnp.zeros_like(vbuf)
+
+    own_copy.wait()
+    for copy in kv_copies:
+        copy.wait()
+
+    def kv_rows(c, carry):
+        for j in range(width // 512):
+            x = g[0, rows_of(c), j * 512 : (j + 1) * 512].astype(F32)
+            gj = gain[:, pl.ds(pl.multiple_of(me * width + j * 512, 512), 512)]
+            nrm[0, :, j * 512 : (j + 1) * 512] = (x * gj).astype(BF16)
+        for r in (3, 1, 2, 0):
+            t = jnp.dot(
+                nrm[0, :, :half], wo[0, :, r * 256 : (r + 1) * 256], preferred_element_type=F32
+            )
+            t += jnp.dot(
+                nrm[0, :, half:],
+                wo[0, :, 1024 + r * 256 : 1024 + (r + 1) * 256],
+                preferred_element_type=F32,
+            )
+            kvp[r, rows_of(c), :] = t
+        return carry
+
+    lax.fori_loop(0, CHUNKS, kv_rows, 0)
+    wo_copies[0].start()
+    kv_a = remote(kvp.at[3], kvr.at[1], kv_s.at[0], kv_r.at[0], d1)
+    kv_b = remote(kvp.at[1], kvr.at[0], kv_s.at[1], kv_r.at[1], d1)
+    kv_x = remote(kxs, kxr, kv_s.at[2], kv_r.at[2], d2)
+    kv_a.start()
+    kv_b.start()
+    kv_a.wait_recv()
+    kxs[...] = (kvp[2] + kvr[1]).astype(BF16)
+    kv_x.start()
+
+    for copy in wq_copies:
+        copy.wait()
+
+    def chunk(c, carry):
+        here = rows_of(c)
+        gather_x(c).wait_recv()
+        forward(c).start()
+        gather_x(c).wait_send()
+        gather_core(c).wait_send()
+
+        @pl.when(c + 2 < CHUNKS)
+        def _():
+            gather_x(c + 2).start()
+            gather_core(c + 2).start()
+
+        row = c * R + lax.broadcasted_iota(jnp.int32, (R, rows), 0)
+        col = lax.broadcasted_iota(jnp.int32, (R, rows), 1)
+        ids_row = jnp.broadcast_to(ids[...].astype(F32), (R, rows))
+        ids_col = jnp.sum(jnp.where(row == col, ids_row, 0.0), axis=1, keepdims=True)
+        same = ids_row == ids_col
+        pos = jnp.sum(jnp.where(same & (col < row), 1.0, 0.0), axis=1, keepdims=True)
+        angle = pos * freq[...]
+        cosine = jnp.cos(angle)
+        sine = jnp.sin(angle) * sign[...]
+        live = ids_col >= 0.0
+        bias = jnp.where(same & (col <= row), 0.0, -1e30)
+
+        gather_core(c).wait_recv()
+        forward(c).wait_recv()
+        squares = jnp.zeros((R, HD), F32)
+        for r in range(4):
+            for j in range(width // 512):
+                x = g[r, here, j * 512 : (j + 1) * 512].astype(F32)
+                gj = gain[:, pl.ds(pl.multiple_of(dev[r] * width + j * 512, 512), 512)]
+                nrm[r, :, j * 512 : (j + 1) * 512] = (x * gj).astype(BF16)
+                xx = x * x
+                for k in range(4):
+                    squares += xx[:, k * HD : (k + 1) * HD]
+        scale = lax.rsqrt(jnp.sum(squares, axis=1, keepdims=True) / D + 1e-05)
+
+        def query(n, carry):
+            cols = pl.ds(pl.multiple_of(n * 256, 256), 256)
+            t = jnp.dot(nrm[0], wq[0, :, cols], preferred_element_type=F32)
+            for r in range(1, 4):
+                t += jnp.dot(nrm[r], wq[r, :, cols], preferred_element_type=F32)
+            t = t * scale
+            t = jnp.concatenate(
+                [turn(t[:, :HD], cosine, sine), turn(t[:, HD:], cosine, sine)], axis=1
+            )
+            qbuf[:, cols] = t.astype(BF16)
+            return carry
+
+        lax.fori_loop(0, heads // 2, query, 0)
+
+        @pl.when(c == 0)
+        def _():
+            kv_b.wait_recv()
+            kv_x.wait_recv()
+
+        kv = (kvp[0, here, :] + kvr[0, here, :] + kxr[here, :].astype(F32)) * scale
+        kbuf[here, :] = turn(kv[:, :HD], cosine, sine).astype(BF16)
+        vbuf[here, :] = kv[:, HD:].astype(BF16)
+
+        def attend(h, carry):
+            for one in range(2):
+                cols = pl.ds(pl.multiple_of(h * 256 + one * HD, HD), HD)
+                s = lax.dot_general(
+                    qbuf[:, cols], kbuf[...], (((1,), (1,)), ((), ())), preferred_element_type=F32
+                )
+                s = s * (HD**-0.5) + bias
+                e = jnp.exp(s - jnp.max(s, axis=1, keepdims=True))
+                total = jnp.maximum(jnp.sum(e, axis=1, keepdims=True), 1.0)
+                p = (e * jnp.where(live, 1.0 / total, 0.0)).astype(BF16)
+                ctx[here, cols] = jnp.dot(p, vbuf[...], preferred_element_type=F32).astype(BF16)
+            return carry
+
+        lax.fori_loop(0, heads // 2, attend, 0)
+
+        send_a = remote(a_out, a_in.at[c], a_s.at[0], a_r.at[c], d1)
+        send_b = remote(b_out, b_in.at[c], b_s.at[0], b_r.at[c], d1)
+        send_x = remote(x_out.at[c], x_in.at[c], x_s.at[c], x_r.at[c], d2)
+
+        @pl.when(c == 0)
+        def _():
+            for r in (3, 1, 2):
+                wo_copies[r].wait()
+
+        @pl.when(c > 0)
+        def _():
+            send_a.wait_send()
+            send_b.wait_send()
+
+        def project(r, n):
+            cols = pl.ds(pl.multiple_of(n * 512, 512), 512)
+            return cols, jnp.dot(ctx[here, :], wo[r, :, cols], preferred_element_type=F32)
+
+        def part_a(n, carry):
+            cols, t = project(3, n)
+            a_out[:, cols] = t.astype(BF16)
+            return carry
+
+        lax.fori_loop(0, width // 512, part_a, 0)
+        send_a.start()
+
+        def part_b(n, carry):
+            cols, t = project(1, n)
+            b_out[:, cols] = t.astype(BF16)
+            return carry
+
+        lax.fori_loop(0, width // 512, part_b, 0)
+        send_b.start()
+        send_a.wait_recv()
+
+        def part_x(n, carry):
+            cols, t = project(2, n)
+            x_out[c, :, cols] = (t + a_in[c, :, cols].astype(F32)).astype(BF16)
+            return carry
+
+        lax.fori_loop(0, width // 512, part_x, 0)
+        send_x.start()
+        return carry
+
+    lax.fori_loop(0, CHUNKS, chunk, 0)
+    wo_copies[0].wait()
+
+    def store(c):
+        return pltpu.make_async_copy(g.at[0, rows_of(c), :], out.at[rows_of(c), :], l_out.at[c])
+
+    def finish(c, carry):
+        here = rows_of(c)
+        remote(b_out, b_in.at[c], b_s.at[0], b_r.at[c], d1).wait_recv()
+
+        def own(n, carry):
+            cols = pl.ds(pl.multiple_of(n * 512, 512), 512)
+            t = jnp.dot(ctx[here, :], wo[0, :, cols], preferred_element_type=F32)
+            acc[:, cols] = t + b_in[c, :, cols].astype(F32) + g[0, here, cols].astype(F32)
+            return carry
+
+        lax.fori_loop(0, width // 512, own, 0)
+        remote(x_out.at[c], x_in.at[c], x_s.at[c], x_r.at[c], d2).wait_recv()
+        for j in range(width // 512):
+            cols = slice(j * 512, (j + 1) * 512)
+            g[0, here, cols] = (acc[:, cols] + x_in[c, :, cols].astype(F32)).astype(BF16)
+        store(c).start()
+        return carry
+
+    lax.fori_loop(0, CHUNKS, finish, 0)
+
+    kv_a.wait_send()
+    kv_b.wait_send()
+    kv_x.wait_send()
+    remote(a_out, a_in.at[0], a_s.at[0], a_r.at[0], d1).wait_send()
+    remote(b_out, b_in.at[0], b_s.at[0], b_r.at[0], d1).wait_send()
+    for c in range(CHUNKS):
+        forward(c).wait_send()
+        remote(x_out.at[c], x_in.at[c], x_s.at[c], x_r.at[c], d2).wait_send()
+        store(c).wait()
+
+
+def fused(hidden_in, norm_gain, w_query, w_keyval, w_out, hyp_ids):
+    rows, width = hidden_in.shape
+    R = rows // CHUNKS
+    qc = w_query.shape[1]
+    exponent = np.arange(HD // 2, dtype=np.float32) * np.float32(2.0 / HD)
+    base = np.power(np.float32(500000.0), -exponent).astype(np.float32)
+    freq = jnp.asarray(np.concatenate([base, base])[None, :])
+    sign = jnp.asarray(np.repeat(np.float32([-1.0, 1.0]), HD // 2)[None, :])
+    vmem = pl.BlockSpec(memory_space=pltpu.VMEM)
+    hbm = pl.BlockSpec(memory_space=pl.ANY)
+    dma = pltpu.SemaphoreType.DMA
+    return pl.pallas_call(
+        kernel,
+        out_shape=jax.ShapeDtypeStruct((rows, width), BF16),
+        in_specs=[hbm, vmem, vmem, vmem, vmem, hbm, hbm, hbm],
+        out_specs=hbm,
+        scratch_shapes=[
+            pltpu.VMEM((4, rows, width), BF16),
+            pltpu.VMEM((4, width, qc), BF16),
+            pltpu.VMEM((4, qc, width), BF16),
+            pltpu.VMEM((4, R, width), BF16),
+            pltpu.VMEM((4, rows, 2 * HD), F32),
+            pltpu.VMEM((2, rows, 2 * HD), F32),
+            pltpu.VMEM((rows, 2 * HD), BF16),
+            pltpu.VMEM((rows, 2 * HD), BF16),
+            pltpu.VMEM((rows, HD), BF16),
+            pltpu.VMEM((rows, HD), BF16),
+            pltpu.VMEM((R, qc), BF16),
+            pltpu.VMEM((rows, qc), BF16),
+            pltpu.VMEM((R, width), BF16),
+            pltpu.VMEM((R, width), BF16),
+            pltpu.VMEM((CHUNKS, R, width), BF16),
+            pltpu.VMEM((CHUNKS, R, width), BF16),
+            pltpu.VMEM((CHUNKS, R, width), BF16),
+            pltpu.VMEM((CHUNKS, R, width), BF16),
+            pltpu.VMEM((R, width), F32),
+            dma((CHUNKS,)), dma((CHUNKS,)), dma((CHUNKS,)),
+            dma((CHUNKS,)), dma((CHUNKS,)), dma((CHUNKS,)),
+            dma((3,)), dma((3,)),
+            dma((1,)), dma((1,)), dma((CHUNKS,)),
+            dma((CHUNKS,)), dma((CHUNKS,)), dma((CHUNKS,)),
+            dma((1,)), dma((16,)), dma((4,)), dma((4,)), dma((CHUNKS,)),
+        ],
+        compiler_params=pltpu.CompilerParams(
+            collective_id=0, has_side_effects=True, vmem_limit_bytes=VMEM_LIMIT
+        ),
+    )(
+        hidden_in, norm_gain.reshape(1, -1), freq, sign, hyp_ids.reshape(1, -1),
+        w_query, w_keyval, w_out,
+    )
+
+
+VMEM_LIMIT = 62 * 1024 * 1024
 
 
 def positions(ids):
@@ -86,8 +430,9 @@
 
 
 def solution(mesh):
+    body = fused if mesh.shape["tensor"] == 4 else shards
     return jax.shard_map(
-        shards,
+        body,
         mesh=mesh,
         in_specs=(
             P(("groups", "dp"), "tensor"),

time: 317 us -> 106 us (0.33)
  waiting for transfers between devices: 228 us -> 0 us
  Pallas kernels: 0 us -> 102 us
  matrix products: 41.7 us -> 0 us
  other arithmetic: 22.4 us -> 0 us
  between operations: 13.3 us -> 0.01 us
  local copies, waits for them, and re-layouts: 11.9 us -> 3.16 us
    reduce_scatter x1 -> x0, waiting for transfers between devices: 126 us -> none  [shards(): lax.psum_scatter(out_term, 'tensor', scatter_dimension=1, tiled=True)]
    pallas_call x0 -> x1, Pallas kernels: none -> 102 us  [fused(): pl.pallas_call(kernel, out_shape=jax.ShapeDtypeStruct((rows, width), BF16...]
    all_gather x1 -> x0, waiting for transfers between devices: 52 us -> none  [shards(): whole = lax.all_gather(hidden_in, 'tensor', axis=1, tiled=True)]
    psum x1 -> x0, waiting for transfers between devices: 48.6 us -> none  [shards(): keyval = lax.psum(kv_term, 'tensor')]
    dot_general x7 -> x0, matrix products: 41.7 us -> none  [the longest x1 14.6 us: shards(): query_raw = jnp.dot(normed, w_query, preferred_element_type=jnp.float32)]
    sub x1 -> x0, other arithmetic: 6.48 us -> none  [shards(): expo = jnp.where(allowed[None], jnp.exp(scores - peak), jnp.float32(0.0))]
    reduce_sum x1 -> x0, other arithmetic: 5.1 us -> none  [shards(): squares = jnp.sum(wide * wide, axis=-1)]
    convert_element_type x2 -> x0, other arithmetic: 4.26 us -> none  [the longest x1 4.18 us: shards(): return (hidden_in.astype(jnp.float32) + summed).astype(jnp.bfloat16)]
  transfers between devices with their start and end apart: 3 -> 0, of which waited for: 3 -> 0; matrix products, arithmetic and copies ran while one was open for 5% -> 0% of each run, Pallas kernels for 0% -> 0%
where the time goes in v1:
time: 106 us
  Pallas kernels  102 us (96%)
  local copies, waits for them, and re-layouts  3.16 us (3%)
    pallas_call x1, Pallas kernels, fused(): pl.pallas_call(kernel, out_shape=jax.ShapeDtypeStruct((rows, width), BF16...  102 us
    unnamed x1, local copies, waits for them, and re-layouts  3.16 us

profile of v1, /device:TPU:0, one launch (start us, length us, event | category | flops | bytes accessed | tf_op | source)
XLA Modules:
  0.0 105.5 jit_solution(12039515015290619688)
XLA Ops:
  0.0 102.4 %shard_map.82 = bf16[512,2048]{1,0:T(8,128)(2,1)} custom-call(bf16[512,2048]{1,0:T(8,128)(2,1)} %hid.1, f32[1,8192]{1,0:T(1,128)} %bitcast.2, f32[1,128]{1,0:T(1,128)} %constant.4.clone.freq, f32[1,128]{1,0:T(1,128)} %constant.5.clone.sign, s32[1,512]{1,0:T(1,128)} %bitcast.3, bf16[8192,1024]{1,0:T(8,128)(2,1)} %wq_h.1, bf16[2048,1024]{1,0:T(8,128)(2,1)} %wkv_h.1, ...), custom_call_target="tpu_custom_call" | custom-call | tf_op jit(solution)/shard_map/pallas_call | solution.py:312
  102.4 3.2 %copy.10 = bf16[512,2048]{1,0:T(8,128)(2,1)} copy(bf16[512,2048]{1,0:T(8,128)(2,1)} %shard_map.82) | data formatting | bytes 4194304

commit v2 on v1

--- a/solution.py
+++ b/solution.py
@@ -24,10 +24,10 @@
 
 def kernel(
     hid, gain, freq, sign, ids, wq_h, wkv_h, wo_h, out,
-    g, wq, wo, nrm, kvp, kvr, kxs, kxr, kbuf, vbuf, qbuf, ctx,
-    a_out, b_out, x_out, a_in, b_in, x_in, acc,
+    far, wq, wo, nrm, kvp, kvr, kxs, kxr, kbuf, vbuf, qbuf, ctx,
+    a_out, b_out, x_out, a_in, b_in, x_in,
     agx_s, agc_s, fwd_s, g1_r, g2_r, g3_r, kv_s, kv_r,
-    a_s, b_s, x_s, a_r, b_r, x_r, l_hid, l_kv, l_wq, l_wo, l_out,
+    a_s, b_s, x_s, a_r, b_r, x_r, l_hid, l_kv, l_wq, l_wo,
 ):
     rows, width = hid.shape
     R = rows // CHUNKS
@@ -39,13 +39,13 @@
     d2 = (1 - chip) * 2 + core
     d3 = 3 - me
     dev = (me, d1, d2, d3)
+    g = (out, far.at[0], far.at[1], far.at[2])
 
     barrier = pltpu.get_barrier_semaphore()
     for other in (d1, d2):
         pl.semaphore_signal(barrier, inc=1, device_id={"tensor": other}, device_id_type=MESH)
 
-    own_copy = pltpu.make_async_copy(hid, g.at[0], l_hid.at[0])
-    own_copy.start()
+    own_copy = pltpu.make_async_copy(hid, out, l_hid.at[0])
     kv_copies = []
     for r in range(4):
         for which in range(2):
@@ -58,10 +58,6 @@
                         l_kv.at[(r * 2 + which) * 2 + h],
                     )
                 )
-    for copy in kv_copies:
-        copy.start()
-
-    pl.semaphore_wait(barrier, 2)
 
     def rows_of(c):
         return pl.ds(pl.multiple_of(c * R, R), R)
@@ -73,18 +69,22 @@
         )
 
     def gather_x(c):
-        return remote(hid.at[rows_of(c), :], g.at[2, rows_of(c), :], agx_s.at[c], g2_r.at[c], d2)
+        return remote(hid.at[rows_of(c), :], far.at[1, rows_of(c), :], agx_s.at[c], g2_r.at[c], d2)
 
     def gather_core(c):
-        return remote(hid.at[rows_of(c), :], g.at[1, rows_of(c), :], agc_s.at[c], g1_r.at[c], d1)
+        return remote(hid.at[rows_of(c), :], far.at[0, rows_of(c), :], agc_s.at[c], g1_r.at[c], d1)
 
     def forward(c):
         return remote(
-            g.at[2, rows_of(c), :], g.at[3, rows_of(c), :], fwd_s.at[c], g3_r.at[c], d1
+            far.at[1, rows_of(c), :], far.at[2, rows_of(c), :], fwd_s.at[c], g3_r.at[c], d1
         )
 
-    for c in range(2):
-        gather_x(c).start()
+    pl.semaphore_wait(barrier, 2)
+    gather_x(0).start()
+    own_copy.start()
+    for copy in kv_copies:
+        copy.start()
+    for c in range(CHUNKS):
         gather_core(c).start()
 
     wq_copies = [
@@ -99,21 +99,18 @@
         )
         for r in range(4)
     ]
-    for copy in wq_copies:
-        copy.start()
-    for r in (3, 1, 2):
-        wo_copies[r].start()
-
     kbuf[...] = jnp.zeros_like(kbuf)
     vbuf[...] = jnp.zeros_like(vbuf)
 
     own_copy.wait()
     for copy in kv_copies:
         copy.wait()
+    for copy in wq_copies:
+        copy.start()
 
     def kv_rows(c, carry):
         for j in range(width // 512):
-            x = g[0, rows_of(c), j * 512 : (j + 1) * 512].astype(F32)
+            x = out[rows_of(c), j * 512 : (j + 1) * 512].astype(F32)
             gj = gain[:, pl.ds(pl.multiple_of(me * width + j * 512, 512), 512)]
             nrm[0, :, j * 512 : (j + 1) * 512] = (x * gj).astype(BF16)
         for r in (3, 1, 2, 0):
@@ -129,12 +126,14 @@
         return carry
 
     lax.fori_loop(0, CHUNKS, kv_rows, 0)
-    wo_copies[0].start()
     kv_a = remote(kvp.at[3], kvr.at[1], kv_s.at[0], kv_r.at[0], d1)
     kv_b = remote(kvp.at[1], kvr.at[0], kv_s.at[1], kv_r.at[1], d1)
     kv_x = remote(kxs, kxr, kv_s.at[2], kv_r.at[2], d2)
     kv_a.start()
     kv_b.start()
+    gather_x(1).start()
+    for r in (3, 1, 2, 0):
+        wo_copies[r].start()
     kv_a.wait_recv()
     kxs[...] = (kvp[2] + kvr[1]).astype(BF16)
     kv_x.start()
@@ -146,13 +145,6 @@
         here = rows_of(c)
         gather_x(c).wait_recv()
         forward(c).start()
-        gather_x(c).wait_send()
-        gather_core(c).wait_send()
-
-        @pl.when(c + 2 < CHUNKS)
-        def _():
-            gather_x(c + 2).start()
-            gather_core(c + 2).start()
 
         row = c * R + lax.broadcasted_iota(jnp.int32, (R, rows), 0)
         col = lax.broadcasted_iota(jnp.int32, (R, rows), 1)
@@ -171,7 +163,7 @@
         squares = jnp.zeros((R, HD), F32)
         for r in range(4):
             for j in range(width // 512):
-                x = g[r, here, j * 512 : (j + 1) * 512].astype(F32)
+                x = g[r][here, j * 512 : (j + 1) * 512].astype(F32)
                 gj = gain[:, pl.ds(pl.multiple_of(dev[r] * width + j * 512, 512), 512)]
                 nrm[r, :, j * 512 : (j + 1) * 512] = (x * gj).astype(BF16)
                 xx = x * x
@@ -193,6 +185,10 @@
 
         lax.fori_loop(0, heads // 2, query, 0)
 
+        @pl.when(c + 2 < CHUNKS)
+        def _():
+            gather_x(c + 2).start()
+
         @pl.when(c == 0)
         def _():
             kv_b.wait_recv()
@@ -202,20 +198,27 @@
         kbuf[here, :] = turn(kv[:, :HD], cosine, sine).astype(BF16)
         vbuf[here, :] = kv[:, HD:].astype(BF16)
 
-        def attend(h, carry):
-            for one in range(2):
-                cols = pl.ds(pl.multiple_of(h * 256 + one * HD, HD), HD)
-                s = lax.dot_general(
-                    qbuf[:, cols], kbuf[...], (((1,), (1,)), ((), ())), preferred_element_type=F32
-                )
-                s = s * (HD**-0.5) + bias
-                e = jnp.exp(s - jnp.max(s, axis=1, keepdims=True))
-                total = jnp.maximum(jnp.sum(e, axis=1, keepdims=True), 1.0)
-                p = (e * jnp.where(live, 1.0 / total, 0.0)).astype(BF16)
-                ctx[here, cols] = jnp.dot(p, vbuf[...], preferred_element_type=F32).astype(BF16)
-            return carry
-
-        lax.fori_loop(0, heads // 2, attend, 0)
+        for upto in range(CHUNKS):
+            keys = (upto + 1) * R
+
+            def attend(h, carry, keys=keys):
+                for one in range(2):
+                    cols = pl.ds(pl.multiple_of(h * 256 + one * HD, HD), HD)
+                    s = lax.dot_general(
+                        qbuf[:, cols], kbuf[:keys, :], (((1,), (1,)), ((), ())),
+                        preferred_element_type=F32,
+                    )
+                    s = s * (HD**-0.5) + bias[:, :keys]
+                    e = jnp.exp(s - jnp.max(s, axis=1, keepdims=True))
+                    total = jnp.maximum(jnp.sum(e, axis=1, keepdims=True), 1.0)
+                    p = (e * jnp.where(live, 1.0 / total, 0.0)).astype(BF16)
+                    t = jnp.dot(p, vbuf[:keys, :], preferred_element_type=F32)
+                    ctx[here, cols] = t.astype(BF16)
+                return carry
+
+            @pl.when(c == upto)
+            def _(attend=attend):
+                lax.fori_loop(0, heads // 2, attend, 0)
 
         send_a = remote(a_out, a_in.at[c], a_s.at[0], a_r.at[c], d1)
         send_b = remote(b_out, b_in.at[c], b_s.at[0], b_r.at[c], d1)
@@ -264,38 +267,44 @@
     lax.fori_loop(0, CHUNKS, chunk, 0)
     wo_copies[0].wait()
 
-    def store(c):
-        return pltpu.make_async_copy(g.at[0, rows_of(c), :], out.at[rows_of(c), :], l_out.at[c])
-
-    def finish(c, carry):
-        here = rows_of(c)
+    def prepare(c):
         remote(b_out, b_in.at[c], b_s.at[0], b_r.at[c], d1).wait_recv()
 
         def own(n, carry):
-            cols = pl.ds(pl.multiple_of(n * 512, 512), 512)
-            t = jnp.dot(ctx[here, :], wo[0, :, cols], preferred_element_type=F32)
-            acc[:, cols] = t + b_in[c, :, cols].astype(F32) + g[0, here, cols].astype(F32)
+            cols = pl.ds(pl.multiple_of(n * 256, 256), 256)
+            t = jnp.dot(ctx[rows_of(c), :], wo[0, :, cols], preferred_element_type=F32)
+            t = t + b_in[c, :, cols].astype(F32) + out[rows_of(c), cols].astype(F32)
+            kvp[(c % 2) * 2 + n // 4, pl.ds(pl.multiple_of((n % 4) * R, R), R), :] = t
             return carry
 
-        lax.fori_loop(0, width // 512, own, 0)
-        remote(x_out.at[c], x_in.at[c], x_s.at[c], x_r.at[c], d2).wait_recv()
-        for j in range(width // 512):
-            cols = slice(j * 512, (j + 1) * 512)
-            g[0, here, cols] = (acc[:, cols] + x_in[c, :, cols].astype(F32)).astype(BF16)
-        store(c).start()
-        return carry
-
-    lax.fori_loop(0, CHUNKS, finish, 0)
+        lax.fori_loop(0, width // 256, own, 0)
 
     kv_a.wait_send()
     kv_b.wait_send()
+    prepare(0)
+
+    def finish(c, carry):
+        @pl.when(c + 1 < CHUNKS)
+        def _():
+            prepare(c + 1)
+
+        remote(x_out.at[c], x_in.at[c], x_s.at[c], x_r.at[c], d2).wait_recv()
+        for n in range(width // 256):
+            cols = slice(n * 256, (n + 1) * 256)
+            t = kvp[(c % 2) * 2 + n // 4, (n % 4) * R : (n % 4 + 1) * R, :]
+            out[rows_of(c), cols] = (t + x_in[c, :, cols].astype(F32)).astype(BF16)
+        return carry
+
+    lax.fori_loop(0, CHUNKS, finish, 0)
+
     kv_x.wait_send()
     remote(a_out, a_in.at[0], a_s.at[0], a_r.at[0], d1).wait_send()
     remote(b_out, b_in.at[0], b_s.at[0], b_r.at[0], d1).wait_send()
     for c in range(CHUNKS):
+        gather_x(c).wait_send()
+        gather_core(c).wait_send()
         forward(c).wait_send()
         remote(x_out.at[c], x_in.at[c], x_s.at[c], x_r.at[c], d2).wait_send()
-        store(c).wait()
 
 
 def fused(hidden_in, norm_gain, w_query, w_keyval, w_out, hyp_ids):
@@ -311,11 +320,11 @@
     dma = pltpu.SemaphoreType.DMA
     return pl.pallas_call(
         kernel,
-        out_shape=jax.ShapeDtypeStruct((rows, width), BF16),
+        out_shape=pltpu.VMEM((rows, width), BF16),
         in_specs=[hbm, vmem, vmem, vmem, vmem, hbm, hbm, hbm],
-        out_specs=hbm,
+        out_specs=vmem,
         scratch_shapes=[
-            pltpu.VMEM((4, rows, width), BF16),
+            pltpu.VMEM((3, rows, width), BF16),
             pltpu.VMEM((4, width, qc), BF16),
             pltpu.VMEM((4, qc, width), BF16),
             pltpu.VMEM((4, R, width), BF16),
@@ -333,13 +342,12 @@
             pltpu.VMEM((CHUNKS, R, width), BF16),
             pltpu.VMEM((CHUNKS, R, width), BF16),
             pltpu.VMEM((CHUNKS, R, width), BF16),
-            pltpu.VMEM((R, width), F32),
             dma((CHUNKS,)), dma((CHUNKS,)), dma((CHUNKS,)),
             dma((CHUNKS,)), dma((CHUNKS,)), dma((CHUNKS,)),
             dma((3,)), dma((3,)),
             dma((1,)), dma((1,)), dma((CHUNKS,)),
             dma((CHUNKS,)), dma((CHUNKS,)), dma((CHUNKS,)),
-            dma((1,)), dma((16,)), dma((4,)), dma((4,)), dma((CHUNKS,)),
+            dma((1,)), dma((16,)), dma((4,)), dma((4,)),
         ],
         compiler_params=pltpu.CompilerParams(
             collective_id=0, has_side_effects=True, vmem_limit_bytes=VMEM_LIMIT
@@ -350,7 +358,7 @@
     )
 
 
-VMEM_LIMIT = 62 * 1024 * 1024
+VMEM_LIMIT = 60 * 1024 * 1024
 
 
 def positions(ids):

time: 106 us -> 103 us (0.972)
  local copies, waits for them, and re-layouts: 3.16 us -> 1.32 us
    unnamed x1, local copies, waits for them, and re-layouts: 3.16 us -> 1.32 us
where the time goes in v2:
time: 103 us
  Pallas kernels  102 us (99%)
  local copies, waits for them, and re-layouts  1.32 us (1%)
    pallas_call x1, Pallas kernels, fused(): pl.pallas_call(kernel, out_shape=pltpu.VMEM((rows, width), BF16), in_spec...  102 us

profile of v2, /device:TPU:0, one launch (start us, length us, event | category | flops | bytes accessed | tf_op | source)
XLA Modules:
  0.0 102.9 jit_solution(14206964465237376002)
XLA Ops:
  0.0 101.6 %shard_map.82 = bf16[512,2048]{1,0:T(8,128)(2,1)S(1)} custom-call(bf16[512,2048]{1,0:T(8,128)(2,1)} %hid.1, f32[1,8192]{1,0:T(1,128)} %bitcast.2, f32[1,128]{1,0:T(1,128)} %constant.4.clone.freq, f32[1,128]{1,0:T(1,128)} %constant.5.clone.sign, s32[1,512]{1,0:T(1,128)} %bitcast.3, bf16[8192,1024]{1,0:T(8,128)(2,1)} %wq_h.1, bf16[2048,1024]{1,0:T(8,128)(2,1)} %wkv_h.1, ...), custom_call_target="tpu_custom_call" | custom-call | tf_op jit(solution)/shard_map/pallas_call | solution.py:321
  101.6 1.3 %copy.10 = bf16[512,2048]{1,0:T(8,128)(2,1)} copy(bf16[512,2048]{1,0:T(8,128)(2,1)S(1)} %shard_map.82) | data formatting | bytes 4194304

commit v3 on v2

--- a/solution.py
+++ b/solution.py
@@ -23,11 +23,11 @@
 
 
 def kernel(
-    hid, gain, freq, sign, ids, wq_h, wkv_h, wo_h, out,
-    far, wq, wo, nrm, kvp, kvr, kxs, kxr, kbuf, vbuf, qbuf, ctx,
+    hid, gain_h, freq_h, ids_h, wq_h, wkv_h, wo_h, out,
+    gain, freq, ids,    far, wq, wo, nrm, kvp, kvr, kxs, kxr, kbuf, vbuf, qbuf, ctx,
     a_out, b_out, x_out, a_in, b_in, x_in,
     agx_s, agc_s, fwd_s, g1_r, g2_r, g3_r, kv_s, kv_r,
-    a_s, b_s, x_s, a_r, b_r, x_r, l_hid, l_kv, l_wq, l_wo,
+    a_s, b_s, x_s, a_r, b_r, x_r, l_small, l_hid, l_kv, l_wq, l_wo,
 ):
     rows, width = hid.shape
     R = rows // CHUNKS
@@ -82,6 +82,12 @@
     pl.semaphore_wait(barrier, 2)
     gather_x(0).start()
     own_copy.start()
+    small = [
+        pltpu.make_async_copy(src, dst, l_small.at[i])
+        for i, (src, dst) in enumerate(((gain_h, gain), (freq_h, freq), (ids_h, ids)))
+    ]
+    for copy in small:
+        copy.start()
     for copy in kv_copies:
         copy.start()
     for c in range(CHUNKS):
@@ -103,6 +109,8 @@
     vbuf[...] = jnp.zeros_like(vbuf)
 
     own_copy.wait()
+    for copy in small:
+        copy.wait()
     for copy in kv_copies:
         copy.wait()
     for copy in wq_copies:
@@ -154,7 +162,9 @@
         pos = jnp.sum(jnp.where(same & (col < row), 1.0, 0.0), axis=1, keepdims=True)
         angle = pos * freq[...]
         cosine = jnp.cos(angle)
-        sine = jnp.sin(angle) * sign[...]
+        sine = jnp.sin(angle)
+        lane = lax.broadcasted_iota(jnp.int32, (R, HD), 1)
+        sine = jnp.where(lane < HD // 2, -sine, sine)
         live = ids_col >= 0.0
         bias = jnp.where(same & (col <= row), 0.0, -1e30)
 
@@ -314,16 +324,18 @@
     exponent = np.arange(HD // 2, dtype=np.float32) * np.float32(2.0 / HD)
     base = np.power(np.float32(500000.0), -exponent).astype(np.float32)
     freq = jnp.asarray(np.concatenate([base, base])[None, :])
-    sign = jnp.asarray(np.repeat(np.float32([-1.0, 1.0]), HD // 2)[None, :])
     vmem = pl.BlockSpec(memory_space=pltpu.VMEM)
     hbm = pl.BlockSpec(memory_space=pl.ANY)
     dma = pltpu.SemaphoreType.DMA
     return pl.pallas_call(
         kernel,
         out_shape=pltpu.VMEM((rows, width), BF16),
-        in_specs=[hbm, vmem, vmem, vmem, vmem, hbm, hbm, hbm],
+        in_specs=[hbm] * 7,
         out_specs=vmem,
         scratch_shapes=[
+            pltpu.VMEM((1, 4 * width), F32),
+            pltpu.VMEM((1, HD), F32),
+            pltpu.VMEM((1, rows), jnp.int32),
             pltpu.VMEM((3, rows, width), BF16),
             pltpu.VMEM((4, width, qc), BF16),
             pltpu.VMEM((4, qc, width), BF16),
@@ -347,13 +359,13 @@
             dma((3,)), dma((3,)),
             dma((1,)), dma((1,)), dma((CHUNKS,)),
             dma((CHUNKS,)), dma((CHUNKS,)), dma((CHUNKS,)),
-            dma((1,)), dma((16,)), dma((4,)), dma((4,)),
+            dma((3,)), dma((1,)), dma((16,)), dma((4,)), dma((4,)),
         ],
         compiler_params=pltpu.CompilerParams(
             collective_id=0, has_side_effects=True, vmem_limit_bytes=VMEM_LIMIT
         ),
     )(
-        hidden_in, norm_gain.reshape(1, -1), freq, sign, hyp_ids.reshape(1, -1),
+        hidden_in, norm_gain.reshape(1, -1), freq, hyp_ids.reshape(1, -1),
         w_query, w_keyval, w_out,
     )
 

time: 103 us -> 102 us (level)
  no operation moved by 1% of the time
where the time goes in v3:
time: 102 us
  Pallas kernels  101 us (99%)
  local copies, waits for them, and re-layouts  1.32 us (1%)
    pallas_call x1, Pallas kernels, fused(): pl.pallas_call(kernel, out_shape=pltpu.VMEM((rows, width), BF16), in_spec...  101 us

profile of v3, /device:TPU:0, one launch (start us, length us, event | category | flops | bytes accessed | tf_op | source)
XLA Modules:
  0.0 102.1 jit_solution(13591780157184830048)
XLA Ops:
  0.0 100.8 %shard_map.73 = bf16[512,2048]{1,0:T(8,128)(2,1)S(1)} custom-call(bf16[512,2048]{1,0:T(8,128)(2,1)} %hid.1, f32[1,8192]{1,0:T(1,128)} %bitcast.2, f32[1,128]{1,0:T(1,128)} %constant.2.clone.freq_h, s32[1,512]{1,0:T(1,128)} %bitcast.3, bf16[8192,1024]{1,0:T(8,128)(2,1)} %wq_h.1, bf16[2048,1024]{1,0:T(8,128)(2,1)} %wkv_h.1, bf16[1024,8192]{1,0:T(8,128)(2,1)} %wo_h.1), custom_call_target="tpu_custom_call" | custom-call | tf_op jit(solution)/shard_map/pallas_call | solution.py:330
  100.8 1.3 %copy.9 = bf16[512,2048]{1,0:T(8,128)(2,1)} copy(bf16[512,2048]{1,0:T(8,128)(2,1)S(1)} %shard_map.73) | data formatting | bytes 4194304
